TPU v7x, 256 devices: a whole 4x4x8 slice. The times are simulated.
256 devices in a mesh: section: 4 (over x), dp: 64 (over z, y, core).
Axes of the slice: x: 4, y: 4, z: 8, core: 2. Of those that a mesh axis runs over, the one named last changes fastest.
Arguments:
- grads: bfloat16 [4, 64, 22, 288, 1024], P('section', 'dp'), may hold values from -6 to 6
- momentum: bfloat16 [4, 22, 294912], P('section', None, 'dp'), may hold values from -48 to 48
- weights: bfloat16 [4, 22, 294912], P('section', None, 'dp'), may hold values from -1.1953125 to 1.1953125
Outputs:
- new_weights: bfloat16 [4, 22, 294912], P('section', None, 'dp')
All inputs are finite; a program needn't handle non-finite values.
Results may differ from a plain program's by a relative error of at most 0.02.
Values may be sent and summed in bfloat16 or wider, within the bound.
A program may use at most 128 MiB of HBM per device.

v0:
```python
import math

import jax
import jax.numpy as jnp
from jax import lax
from jax.experimental import pallas as pl
from jax.experimental.pallas import tpu as pltpu
from jax.sharding import PartitionSpec as P

ITERS = 5
QUINTIC_A = 3.4445
QUINTIC_B = -4.775
QUINTIC_C = 2.0315
MOMENTUM_DECAY = 0.95
LEARN_RATE = 0.5
DECAY_RATE = 0.1
EPSILON = 1e-07

NZ, NY = 8, 4
MATRICES, HEIGHT, BREADTH = 22, 288, 1024
HALF = MATRICES // 2
GROUPS = 64
PORTION = HEIGHT * BREADTH // GROUPS
STRIPS = PORTION // 128
STRIP_ROWS = 48
WINDOW = 32
ROUNDS = 6
ROWS = HEIGHT // ROUNDS
LOW = (0, 384)
WIDTH = (384, 640)
MESH = pl.DeviceIdType.MESH
F32, BF16 = jnp.float32, jnp.bfloat16


def place(dp):
    return dp // 8, lax.rem(dp // 2, NY), lax.rem(dp, 2)


def owner_z(j, c):
    return lax.rem(j + 4 * c, NZ)


def owner_y(j, c):
    return lax.rem(j + j // 8 + 2 * c, NY)


def owned_at(z, y, c):
    v = lax.rem(z + NZ - 4 * c, NZ)
    first = owner_y(v, c) == y
    second = jnp.logical_and(v < 3, owner_y(v + 8, c) == y)
    return jnp.minimum(jnp.where(first, v, v + 8), HALF - 1), jnp.logical_or(first, second)


def candidates(axis, d, z, y, c):
    if axis == 0:
        u = lax.rem(z + d + NZ - 4 * c, NZ)
        return [(u, None), (jnp.minimum(u + 8, HALF - 1), u < 3)]
    u = lax.rem(y + d + NY - 2 * c, NY)
    return [(u, None), (u + 4, None), (jnp.minimum(u + 7, HALF - 1), u >= 1)]


def guarded(valid, body):
    if valid is None:
        body()
    else:
        pl.when(valid)(body)


def roles(axis, d):
    n = NZ if axis == 0 else NY
    far = n // 2
    up, down = 2 * axis, 2 * axis + 1
    receives, sends = [], []
    if d < far - 1:
        receives.append((up, None))
    if d == far - 1:
        receives.append((up, 0))
    if d == 0 or d > far + 1:
        receives.append((down, None))
    if d == far + 1:
        receives.append((down, 1))
    if 1 <= d < far:
        sends.append((up, None))
    if d == far:
        sends += [(up, 0), (down, 1)]
    if d > far:
        sends.append((down, None))
    return receives, sends


ORDER = (
    (1, 0, 4, 0), (1, 1, 2, 0),
    (1, 0, 3, 1), (1, 0, 5, 1), (1, 1, 1, 1), (1, 1, 3, 1),
    (1, 0, 2, 2), (1, 0, 6, 2), (1, 1, 0, 2), (2, 0, 4, 2),
    (1, 0, 1, 3), (1, 0, 7, 3), (2, 0, 3, 3), (2, 0, 5, 3),
    (1, 0, 0, 4), (2, 1, 2, 4), (2, 0, 2, 4), (2, 0, 6, 4),
    (2, 1, 1, 5), (2, 1, 3, 5), (2, 0, 1, 5), (2, 0, 7, 5),
    (2, 1, 0, 6), (2, 0, 0, 6),
)
LAG = 6


def kernel(
    grads, momentum, weights, out, own, other, box, shares, window, current, flat, pieces, got, wide,
    load_sem, cross_send, cross_recv, send_sem, recv_sem, share_sem, piece_send, piece_recv,
):
    section = lax.axis_index("section")
    me = lax.axis_index("dp")
    z, y, c = place(me)
    mine, is_owner = owned_at(z, y, c)
    is_guest = jnp.logical_not(is_owner)

    def device(nz, ny, nc):
        return (section, (nz * NY + ny) * 2 + nc)

    targets = (
        device(lax.rem(z + 1, NZ), y, c),
        device(lax.rem(z + NZ - 1, NZ), y, c),
        device(z, lax.rem(y + 1, NY), c),
        device(z, lax.rem(y + NY - 1, NY), c),
    )
    partner = device(z, y, 1 - c)

    def rows(k):
        return pl.ds(pl.multiple_of(ROWS * k, 16), ROWS)

    def load(k):
        return pltpu.make_async_copy(
            grads.at[pl.ds(HALF * c, HALF), rows(k)], own.at[:, rows(k)], load_sem.at[k]
        )

    def cross(k):
        return pltpu.make_async_remote_copy(
            src_ref=grads.at[pl.ds(HALF * (1 - c), HALF), rows(k)],
            dst_ref=other.at[:, rows(k)],
            send_sem=cross_send.at[k],
            recv_sem=cross_recv.at[k],
            device_id=partner,
            device_id_type=MESH,
        )

    def hop(j, k, t, way):
        part = (rows(k), pl.ds(LOW[t], WIDTH[t]))
        return pltpu.make_async_remote_copy(
            src_ref=own.at[j, part[0], part[1]],
            dst_ref=box.at[way, j, part[0], part[1]],
            send_sem=send_sem,
            recv_sem=recv_sem.at[way, k, j, t],
            device_id=targets[way],
            device_id_type=MESH,
        )

    for k in range(ROUNDS):
        load(k).start()

    barrier = pltpu.get_barrier_semaphore()
    for target in targets + (partner,):
        pl.semaphore_signal(barrier, inc=1, device_id=target, device_id_type=MESH)

    shares[c, 0:MATRICES, :] = momentum[...].astype(F32)

    pl.semaphore_wait(barrier, 5)

    exchange = pltpu.make_async_remote_copy(
        src_ref=shares.at[c],
        dst_ref=shares.at[c],
        send_sem=share_sem.at[0],
        recv_sem=share_sem.at[1],
        device_id=partner,
        device_id_type=MESH,
    )
    exchange.start()
    for k in range(ROUNDS):
        cross(k).start()

    line = 9 * (me // 2)
    base = jnp.minimum(16 * (line // 16), HEIGHT - WINDOW)
    shift = line - base
    window[...] = jnp.zeros_like(window)
    exchange.wait()
    for core in range(2):

        @pl.when(c == core)
        def _():
            for source in range(2):
                for k in range(STRIPS):
                    at = STRIPS * source + k
                    window[at % 8, pl.ds(shift + at // 8, HALF, stride=WINDOW), :] = shares[
                        source, HALF * core : HALF * (core + 1), 128 * k : 128 * (k + 1)
                    ]

    scale = MOMENTUM_DECAY * MOMENTUM_DECAY / (1.0 + MOMENTUM_DECAY)

    def combine(k):
        load(k).wait()
        cross(k).wait_recv()

        def add(j, carry):
            own[j, rows(k), :] = (
                own[j, rows(k), :].astype(F32) + other[j, rows(k), :].astype(F32)
            ).astype(BF16)
            return carry

        lax.fori_loop(0, HALF, add, 0)
        for part in range(WINDOW // 16):
            top = base + 16 * part

            @pl.when(top // ROWS == k)
            def _():
                r = pl.ds(pl.multiple_of(top, 16), 16)

                def blend(j, carry):
                    from_window = pl.ds(pl.multiple_of(WINDOW * j + 16 * part, 16), 16)
                    for block in range(8):
                        lanes = pl.ds(128 * block, 128)
                        own[j, r, lanes] = (
                            own[j, r, lanes].astype(F32) + scale * window[block, from_window, :]
                        ).astype(BF16)
                    return carry

                lax.fori_loop(0, HALF, blend, 0)

    steps = []
    for phase, axis, d, lag in ORDER:
        if phase == 1:
            found = candidates(axis, d, z, y, c)
        elif axis == 0:
            found = [owned_at(lax.rem(z + d, NZ), y, c)]
        else:
            found = [owned_at(z, lax.rem(y + d, NY), c)]
        for j, valid in found:
            steps.append((axis if phase == 1 else 1 - axis, j, valid, lag, *roles(axis, d)))

    def step(k, parity, t, j, receives, sends):
        part = (rows(k), pl.ds(LOW[t], WIDTH[t]))

        def take(ways):
            for way in ways:
                hop(j, k, t, way).wait_recv()
            total = own[j, part[0], part[1]].astype(F32)
            for way in ways:
                total = total + box[way, j, part[0], part[1]].astype(F32)
            own[j, part[0], part[1]] = total.astype(BF16)

        always = [way for way, when in receives if when is None]
        if always:
            take(always)
        for way, when in receives:
            if when is not None:
                pl.when(parity == when)(lambda way=way: take([way]))
        for way, when in sends:
            guarded(None if when is None else parity == when, lambda way=way: hop(j, k, t, way).start())

    combine(0)

    def body(i, carry):
        for t, j, valid, lag, receives, sends in steps:
            k = i - lag
            live = jnp.logical_and(k >= 0, k < ROUNDS)
            if valid is not None:
                live = jnp.logical_and(live, valid)
            pl.when(live)(
                lambda k=k, t=t, j=j, receives=receives, sends=sends: step(
                    k, lax.rem(k + c, 2), t, j, receives, sends
                )
            )

        @pl.when(i + 1 < ROUNDS)
        def _():
            combine(i + 1)

        return carry

    lax.fori_loop(0, ROUNDS + LAG, body, 0)

    slot = HALF * c + mine

    def share(distance):
        to = lax.rem(me + distance, GROUPS)
        return pltpu.make_async_remote_copy(
            src_ref=pieces.at[to],
            dst_ref=got.at[slot],
            send_sem=piece_send,
            recv_sem=piece_recv,
            device_id=(section, to),
            device_id_type=MESH,
        )

    @pl.when(is_owner)
    def _():
        blended = (1.0 + MOMENTUM_DECAY) * own[mine].astype(F32)
        norm = jnp.sqrt(jnp.sum(blended * blended, keepdims=True)) + EPSILON
        current[...] = (blended / norm).astype(BF16)

        def newton(_, carry):
            x = current[...]
            gram = lax.dot_general(
                x, x, (((1,), (1,)), ((), ())), preferred_element_type=F32
            ).astype(BF16)
            square = jnp.dot(gram, gram, preferred_element_type=F32)
            polynomial = (QUINTIC_B * gram.astype(F32) + QUINTIC_C * square).astype(BF16)
            mixed = jnp.dot(polynomial, x, preferred_element_type=F32)
            current[...] = (QUINTIC_A * x.astype(F32) + mixed).astype(BF16)
            return carry

        lax.fori_loop(0, ITERS, newton, 0)
        for k in range(8):
            flat[pl.ds(k, HEIGHT, stride=8), :] = current[:, 128 * k : 128 * (k + 1)].astype(F32)

        def cut(pair, carry):
            both = flat[pl.ds(pl.multiple_of(2 * STRIPS * pair, 8), 2 * STRIPS), :]
            pad = jnp.zeros((STRIP_ROWS - STRIPS, 128), F32)
            pieces[2 * pair] = jnp.concatenate([both[:STRIPS], pad]).astype(BF16)
            pieces[2 * pair + 1] = jnp.concatenate([both[STRIPS:], pad]).astype(BF16)
            return carry

        lax.fori_loop(0, GROUPS // 2, cut, 0)

        def send(distance, carry):
            share(distance).start()
            return carry

        lax.fori_loop(1, GROUPS, send, 0)
        got[slot] = pieces[me]

    for k in range(ROUNDS):
        cross(k).wait_send()

    def sent(number):
        pltpu.make_async_copy(own.at[pl.ds(0, number)], own.at[pl.ds(0, number)], send_sem).wait()

    def arrived(number):
        pltpu.make_async_copy(
            got.at[pl.ds(0, number)], got.at[pl.ds(0, number)], piece_recv
        ).wait()

    @pl.when(is_owner)
    def _():
        sent(HALF - 1)
        arrived(MATRICES - 1)

    @pl.when(is_guest)
    def _():
        sent(HALF)
        arrived(MATRICES)

    for m in range(MATRICES):
        wide[STRIP_ROWS * m : STRIP_ROWS * (m + 1), :] = got[m].astype(F32)
    factor = 0.2 * math.sqrt(max(HEIGHT, BREADTH))
    for k in range(STRIPS):
        lanes = slice(128 * k, 128 * (k + 1))
        update = wide[pl.ds(k, MATRICES, stride=STRIP_ROWS), :]
        out[:, lanes] = (
            weights[:, lanes].astype(F32) * (1.0 - LEARN_RATE * DECAY_RATE)
            - LEARN_RATE * factor * update
        ).astype(BF16)

    @pl.when(is_owner)
    def _():
        pltpu.make_async_copy(
            pieces.at[pl.ds(0, GROUPS - 1)], pieces.at[pl.ds(0, GROUPS - 1)], piece_send
        ).wait()


def local(grads, momentum, weights):
    matrix = (HALF, HEIGHT, BREADTH)
    dma = pltpu.SemaphoreType.DMA
    return pl.pallas_call(
        kernel,
        out_shape=jax.ShapeDtypeStruct((MATRICES, PORTION), BF16),
        in_specs=[pl.BlockSpec(memory_space=pl.ANY)] + [pl.BlockSpec(memory_space=pltpu.VMEM)] * 2,
        out_specs=pl.BlockSpec(memory_space=pltpu.VMEM),
        scratch_shapes=[
            pltpu.VMEM(matrix, BF16),
            pltpu.VMEM(matrix, BF16),
            pltpu.VMEM((4, *matrix), BF16),
            pltpu.VMEM((2, 24, PORTION), F32),
            pltpu.VMEM((8, HALF * WINDOW, 128), F32),
            pltpu.VMEM((HEIGHT, BREADTH), BF16),
            pltpu.VMEM((GROUPS * STRIPS, 128), F32),
            pltpu.VMEM((GROUPS, STRIP_ROWS, 128), BF16),
            pltpu.VMEM((MATRICES, STRIP_ROWS, 128), BF16),
            pltpu.VMEM((MATRICES * STRIP_ROWS, 128), F32),
            dma((ROUNDS,)),
            dma((ROUNDS,)),
            dma((ROUNDS,)),
            dma,
            dma((4, ROUNDS, HALF, 2)),
            dma((2,)),
            dma,
            dma,
        ],
        compiler_params=pltpu.CompilerParams(
            collective_id=0, has_side_effects=True, vmem_limit_bytes=56 << 20
        ),
        name="muon_step",
    )(grads[0, 0], momentum[0], weights[0])[None]


def solution(mesh):
    placed = (
        P("section", "dp", None, None, None),
        P("section", None, "dp"),
        P("section", None, "dp"),
    )
    return jax.shard_map(
        local, mesh=mesh, in_specs=placed, out_specs=P("section", None, "dp"), check_vma=False
    )
```

profile of v0, /device:TPU:1, one launch (start us, length us, event | category | flops | bytes accessed | tf_op | source)
XLA Modules:
  0.0 88.5 jit_solution(17006017052066558218)
XLA Ops:
  0.0 86.8 %muon_step.1 = bf16[22,4608]{1,0:T(8,128)(2,1)} custom-call(bf16[22,288,1024]{2,1,0:T(8,128)(2,1)} %bitcast.4, bf16[22,4608]{1,0:T(8,128)(2,1)} %bitcast.6, bf16[22,4608]{1,0:T(8,128)(2,1)} %bitcast.7), custom_call_target="tpu_custom_call" | custom-call | tf_op jit(solution)/shard_map/muon_step/pallas_call | solution.py:368
  86.8 1.6 %copy.5 = bf16[1,22,4608]{2,1,0:T(8,128)(2,1)} copy(bf16[1,22,4608]{2,1,0:T(8,128)(2,1)} %bitcast.5) | data formatting | bytes 405504
where the time goes:
time: 88.8 us; the launch traced here: 88.5 us
  Pallas kernels  86.8 us (98%)
  local copies, waits for them, and re-layouts  1.64 us (2%)
    pallas_call x1, Pallas kernels, local(): pl.pallas_call(kernel, out_shape=jax.ShapeDtypeStruct((MATRICES, PORTION)...  86.8 us

commit v1 on v0

--- a/solution.py
+++ b/solution.py
@@ -24,6 +24,7 @@
 STRIPS = PORTION // 128
 STRIP_ROWS = 48
 WINDOW = 32
+QUARTER = HEIGHT // 4
 ROUNDS = 6
 ROWS = HEIGHT // ROUNDS
 LOW = (0, 384)
@@ -66,43 +67,60 @@
         pl.when(valid)(body)
 
 
-def roles(axis, d):
+Z_UP, Z_DOWN, Y_UP, Y_DOWN, Z_UP_TWO, Z_DOWN_TWO, Y_UP_TWO = range(7)
+FAR = 4
+
+
+def roles(phase, axis, d):
     n = NZ if axis == 0 else NY
     far = n // 2
     up, down = 2 * axis, 2 * axis + 1
+    if phase == 2 and axis == 1:
+        if d == 0:
+            return [(up, None), (down, None), (FAR, None)], []
+        if d == far:
+            return [], [(Y_UP_TWO, FAR, None)]
+        return [], [(up, up, None) if d < far else (down, down, None)]
     receives, sends = [], []
     if d < far - 1:
         receives.append((up, None))
-    if d == far - 1:
-        receives.append((up, 0))
     if d == 0 or d > far + 1:
         receives.append((down, None))
-    if d == far + 1:
-        receives.append((down, 1))
+    if phase == 1:
+        if d == far - 1:
+            receives.append((up, 0))
+        if d == far + 1:
+            receives.append((down, 1))
+    else:
+        if d == far - 2:
+            receives.append((down, 0))
+        if d == far + 2:
+            receives.append((up, 1))
     if 1 <= d < far:
-        sends.append((up, None))
-    if d == far:
-        sends += [(up, 0), (down, 1)]
+        sends.append((up, up, None))
+    if d == far and phase == 1:
+        sends += [(up, up, 0), (down, down, 1)]
+    if d == far and phase == 2:
+        sends += [(Z_UP_TWO, down, 0), (Z_DOWN_TWO, up, 1)]
     if d > far:
-        sends.append((down, None))
+        sends.append((down, down, None))
     return receives, sends
 
 
 ORDER = (
     (1, 0, 4, 0), (1, 1, 2, 0),
     (1, 0, 3, 1), (1, 0, 5, 1), (1, 1, 1, 1), (1, 1, 3, 1),
-    (1, 0, 2, 2), (1, 0, 6, 2), (1, 1, 0, 2), (2, 0, 4, 2),
-    (1, 0, 1, 3), (1, 0, 7, 3), (2, 0, 3, 3), (2, 0, 5, 3),
-    (1, 0, 0, 4), (2, 1, 2, 4), (2, 0, 2, 4), (2, 0, 6, 4),
-    (2, 1, 1, 5), (2, 1, 3, 5), (2, 0, 1, 5), (2, 0, 7, 5),
-    (2, 1, 0, 6), (2, 0, 0, 6),
+    (1, 0, 2, 2), (1, 0, 6, 2), (1, 1, 0, 2), (2, 0, 4, 2), (2, 0, 3, 2), (2, 0, 5, 2),
+    (1, 0, 1, 3), (1, 0, 7, 3), (2, 0, 2, 3), (2, 0, 6, 3),
+    (1, 0, 0, 4), (2, 1, 2, 4), (2, 1, 1, 4), (2, 1, 3, 4), (2, 0, 1, 4), (2, 0, 7, 4),
+    (2, 1, 0, 5), (2, 0, 0, 5),
 )
-LAG = 6
+LAG = 5
 
 
 def kernel(
-    grads, momentum, weights, out, own, other, box, shares, window, current, flat, pieces, got, wide,
-    load_sem, cross_send, cross_recv, send_sem, recv_sem, share_sem, piece_send, piece_recv,
+    grads, momentum, weights, out, own, other, box, shares, window, near, current, last, scaled, flat, pieces, got, wide,
+    load_sem, cross_send, cross_recv, send_sem, recv_sem, share_sem, near_sem, piece_send, piece_recv,
 ):
     section = lax.axis_index("section")
     me = lax.axis_index("dp")
@@ -118,6 +136,9 @@
         device(lax.rem(z + NZ - 1, NZ), y, c),
         device(z, lax.rem(y + 1, NY), c),
         device(z, lax.rem(y + NY - 1, NY), c),
+        device(lax.rem(z + 2, NZ), y, c),
+        device(lax.rem(z + NZ - 2, NZ), y, c),
+        device(z, lax.rem(y + 2, NY), c),
     )
     partner = device(z, y, 1 - c)
 
@@ -139,14 +160,14 @@
             device_id_type=MESH,
         )
 
-    def hop(j, k, t, way):
+    def hop(j, k, t, target, way):
         part = (rows(k), pl.ds(LOW[t], WIDTH[t]))
         return pltpu.make_async_remote_copy(
             src_ref=own.at[j, part[0], part[1]],
-            dst_ref=box.at[way, j, part[0], part[1]],
+            dst_ref=near.at[part[0], :] if way == FAR else box.at[way, j, part[0], part[1]],
             send_sem=send_sem,
-            recv_sem=recv_sem.at[way, k, j, t],
-            device_id=targets[way],
+            recv_sem=near_sem.at[k] if way == FAR else recv_sem.at[way, k, j, t],
+            device_id=targets[target],
             device_id_type=MESH,
         )
 
@@ -154,7 +175,7 @@
         load(k).start()
 
     barrier = pltpu.get_barrier_semaphore()
-    for target in targets + (partner,):
+    for target in targets[:4] + (partner,):
         pl.semaphore_signal(barrier, inc=1, device_id=target, device_id_type=MESH)
 
     shares[c, 0:MATRICES, :] = momentum[...].astype(F32)
@@ -229,17 +250,20 @@
         else:
             found = [owned_at(z, lax.rem(y + d, NY), c)]
         for j, valid in found:
-            steps.append((axis if phase == 1 else 1 - axis, j, valid, lag, *roles(axis, d)))
+            steps.append((axis if phase == 1 else 1 - axis, j, valid, lag, *roles(phase, axis, d)))
 
     def step(k, parity, t, j, receives, sends):
         part = (rows(k), pl.ds(LOW[t], WIDTH[t]))
 
         def take(ways):
             for way in ways:
-                hop(j, k, t, way).wait_recv()
+                hop(j, k, t, 0, way).wait_recv()
             total = own[j, part[0], part[1]].astype(F32)
             for way in ways:
-                total = total + box[way, j, part[0], part[1]].astype(F32)
+                if way == FAR:
+                    total = total + near[part[0], :].astype(F32)
+                else:
+                    total = total + box[way, j, part[0], part[1]].astype(F32)
             own[j, part[0], part[1]] = total.astype(BF16)
 
         always = [way for way, when in receives if when is None]
@@ -248,8 +272,11 @@
         for way, when in receives:
             if when is not None:
                 pl.when(parity == when)(lambda way=way: take([way]))
-        for way, when in sends:
-            guarded(None if when is None else parity == when, lambda way=way: hop(j, k, t, way).start())
+        for target, way, when in sends:
+            guarded(
+                None if when is None else parity == when,
+                lambda target=target, way=way: hop(j, k, t, target, way).start(),
+            )
 
     combine(0)
 
@@ -275,8 +302,7 @@
 
     slot = HALF * c + mine
 
-    def share(distance):
-        to = lax.rem(me + distance, GROUPS)
+    def share(to):
         return pltpu.make_async_remote_copy(
             src_ref=pieces.at[to],
             dst_ref=got.at[slot],
@@ -303,24 +329,43 @@
             current[...] = (QUINTIC_A * x.astype(F32) + mixed).astype(BF16)
             return carry
 
-        lax.fori_loop(0, ITERS, newton, 0)
-        for k in range(8):
-            flat[pl.ds(k, HEIGHT, stride=8), :] = current[:, 128 * k : 128 * (k + 1)].astype(F32)
-
-        def cut(pair, carry):
-            both = flat[pl.ds(pl.multiple_of(2 * STRIPS * pair, 8), 2 * STRIPS), :]
+        lax.fori_loop(0, ITERS - 1, newton, 0)
+        x = current[...]
+        gram = lax.dot_general(
+            x, x, (((1,), (1,)), ((), ())), preferred_element_type=F32
+        ).astype(BF16)
+        square = jnp.dot(gram, gram, preferred_element_type=F32)
+        last[...] = QUINTIC_B * gram.astype(F32) + QUINTIC_C * square
+        scaled[...] = QUINTIC_A * x.astype(F32)
+
+        def quarter(i, carry):
+            ahead = jnp.where(i == 0, 2, jnp.where(i == 1, 1, jnp.where(i == 2, 3, 0)))
+            q = lax.rem(z // 2 + ahead, 4)
+            r = pl.ds(pl.multiple_of(QUARTER * q, 8), QUARTER)
+            mixed = jnp.dot(last[r, :].astype(BF16), current[...], preferred_element_type=F32)
+            new = scaled[r, :] + mixed
+            for k in range(8):
+                flat[pl.ds(k, QUARTER, stride=8), :] = new[:, 128 * k : 128 * (k + 1)]
             pad = jnp.zeros((STRIP_ROWS - STRIPS, 128), F32)
-            pieces[2 * pair] = jnp.concatenate([both[:STRIPS], pad]).astype(BF16)
-            pieces[2 * pair + 1] = jnp.concatenate([both[STRIPS:], pad]).astype(BF16)
+            for pair in range(8):
+                both = flat[2 * STRIPS * pair : 2 * STRIPS * (pair + 1), :]
+                to = 16 * q + 2 * pair
+                pieces[to] = jnp.concatenate([both[:STRIPS], pad]).astype(BF16)
+                pieces[to + 1] = jnp.concatenate([both[STRIPS:], pad]).astype(BF16)
+
+            def send(e, carry):
+                to = 16 * q + e
+
+                @pl.when(to != me)
+                def _():
+                    share(to).start()
+
+                return carry
+
+            lax.fori_loop(0, 16, send, 0)
             return carry
 
-        lax.fori_loop(0, GROUPS // 2, cut, 0)
-
-        def send(distance, carry):
-            share(distance).start()
-            return carry
-
-        lax.fori_loop(1, GROUPS, send, 0)
+        lax.fori_loop(0, 4, quarter, 0)
         got[slot] = pieces[me]
 
     for k in range(ROUNDS):
@@ -376,8 +421,11 @@
             pltpu.VMEM((4, *matrix), BF16),
             pltpu.VMEM((2, 24, PORTION), F32),
             pltpu.VMEM((8, HALF * WINDOW, 128), F32),
+            pltpu.VMEM((HEIGHT, WIDTH[0]), BF16),
             pltpu.VMEM((HEIGHT, BREADTH), BF16),
-            pltpu.VMEM((GROUPS * STRIPS, 128), F32),
+            pltpu.VMEM((HEIGHT, HEIGHT), F32),
+            pltpu.VMEM((HEIGHT, BREADTH), F32),
+            pltpu.VMEM((QUARTER * 8, 128), F32),
             pltpu.VMEM((GROUPS, STRIP_ROWS, 128), BF16),
             pltpu.VMEM((MATRICES, STRIP_ROWS, 128), BF16),
             pltpu.VMEM((MATRICES * STRIP_ROWS, 128), F32),
@@ -387,6 +435,7 @@
             dma,
             dma((4, ROUNDS, HALF, 2)),
             dma((2,)),
+            dma((ROUNDS,)),
             dma,
             dma,
         ],

time: 88.8 us -> 86.5 us (0.974)
  Pallas kernels: 86.8 us -> 84.7 us
    pallas_call x1, Pallas kernels: 86.8 us -> 84.7 us  [local(): pl.pallas_call(kernel, out_shape=jax.ShapeDtypeStruct((MATRICES, PORTION)...]
where the time goes in v1:
time: 86.5 us; the launch traced here: 86.3 us
  Pallas kernels  84.7 us (98%)
  local copies, waits for them, and re-layouts  1.64 us (2%)
    pallas_call x1, Pallas kernels, local(): pl.pallas_call(kernel, out_shape=jax.ShapeDtypeStruct((MATRICES, PORTION)...  84.7 us

profile of v1, /device:TPU:1, one launch (start us, length us, event | category | flops | bytes accessed | tf_op | source)
XLA Modules:
  0.0 86.3 jit_solution(8238700217866930819)
XLA Ops:
  0.0 84.7 %muon_step.1 = bf16[22,4608]{1,0:T(8,128)(2,1)} custom-call(bf16[22,288,1024]{2,1,0:T(8,128)(2,1)} %bitcast.4, bf16[22,4608]{1,0:T(8,128)(2,1)} %bitcast.6, bf16[22,4608]{1,0:T(8,128)(2,1)} %bitcast.7), custom_call_target="tpu_custom_call" | custom-call | tf_op jit(solution)/shard_map/muon_step/pallas_call | solution.py:413
  84.7 1.6 %copy.5 = bf16[1,22,4608]{2,1,0:T(8,128)(2,1)} copy(bf16[1,22,4608]{2,1,0:T(8,128)(2,1)} %bitcast.5) | data formatting | bytes 405504

commit v2 on v1

--- a/solution.py
+++ b/solution.py
@@ -178,6 +178,7 @@
     for target in targets[:4] + (partner,):
         pl.semaphore_signal(barrier, inc=1, device_id=target, device_id_type=MESH)
 
+    window[...] = jnp.zeros_like(window)
     shares[c, 0:MATRICES, :] = momentum[...].astype(F32)
 
     pl.semaphore_wait(barrier, 5)
@@ -197,7 +198,6 @@
     line = 9 * (me // 2)
     base = jnp.minimum(16 * (line // 16), HEIGHT - WINDOW)
     shift = line - base
-    window[...] = jnp.zeros_like(window)
     exchange.wait()
     for core in range(2):
 
@@ -218,8 +218,8 @@
 
         def add(j, carry):
             own[j, rows(k), :] = (
-                own[j, rows(k), :].astype(F32) + other[j, rows(k), :].astype(F32)
-            ).astype(BF16)
+                own[j, rows(k), :] + other[j, rows(k), :]
+            )
             return carry
 
         lax.fori_loop(0, HALF, add, 0)
@@ -362,7 +362,7 @@
 
                 return carry
 
-            lax.fori_loop(0, 16, send, 0)
+            lax.fori_loop(0, 16, send, 0, unroll=True)
             return carry
 
         lax.fori_loop(0, 4, quarter, 0)

time: 86.5 us -> 86.2 us (level)
  no operation moved by 1% of the time
where the time goes in v2:
time: 86.2 us; the launch traced here: 86.1 us
  Pallas kernels  84.5 us (98%)
  local copies, waits for them, and re-layouts  1.64 us (2%)
    pallas_call x1, Pallas kernels, local(): pl.pallas_call(kernel, out_shape=jax.ShapeDtypeStruct((MATRICES, PORTION)...  84.5 us

profile of v2, /device:TPU:1, one launch (start us, length us, event | category | flops | bytes accessed | tf_op | source)
XLA Modules:
  0.0 86.1 jit_solution(15011771212493295475)
XLA Ops:
  0.0 84.5 %muon_step.1 = bf16[22,4608]{1,0:T(8,128)(2,1)} custom-call(bf16[22,288,1024]{2,1,0:T(8,128)(2,1)} %bitcast.4, bf16[22,4608]{1,0:T(8,128)(2,1)} %bitcast.6, bf16[22,4608]{1,0:T(8,128)(2,1)} %bitcast.7), custom_call_target="tpu_custom_call" | custom-call | tf_op jit(solution)/shard_map/muon_step/pallas_call | solution.py:413
  84.5 1.6 %copy.5 = bf16[1,22,4608]{2,1,0:T(8,128)(2,1)} copy(bf16[1,22,4608]{2,1,0:T(8,128)(2,1)} %bitcast.5) | data formatting | bytes 405504
